TPU v7x, 32 devices: a whole 2x2x4 slice. The times are simulated.
32 devices in a mesh: view: 4 (over y, x), tile: 8 (over z, core).
Axes of the slice: x: 2, y: 2, z: 4, core: 2. Of those that a mesh axis runs over, the one named last changes fastest.
Arguments:
- estimate: float32 [64, 256, 128], P('tile', 'view'), may hold values from 0.5 to 1.5
- images: float32 [4, 64, 256, 128], P('view', 'tile'), may hold values from 0.25 to 4
- taps_first: float32 [4, 5], P('view'), may hold values from 0.1 to 1
- taps_second: float32 [4, 7], P('view'), may hold values from 0.1 to 1
- taps_axial: float32 [4, 33], P('view'), may hold values from 0.02 to 0.2
Outputs:
- deconvolved: float32 [64, 256, 128], P('tile', 'view')
All inputs are finite; a program needn't handle non-finite values.
Results may differ from a plain program's by a relative error of at most 0.0001.
Values sent between devices are 32-bit elements; how exact they have to be, the bound alone decides.
A program may use at most 64 MiB of HBM per device.

v0:
```python
import jax
import jax.numpy as jnp
from jax import lax
from jax.sharding import PartitionSpec as P

ITERS = 2


def extended(cells, sides, width):
    for axis, dim in sides:
        count = lax.axis_size(axis)
        ends = count - 1
        head = lax.slice_in_dim(cells, 0, width, axis=dim)
        tail = lax.slice_in_dim(cells, cells.shape[dim] - width, cells.shape[dim], axis=dim)
        cells = jnp.concatenate(
            [
                lax.ppermute(tail, axis, [(i, (i + 1) % count) for i in range(ends)]),
                cells,
                lax.ppermute(head, axis, [((i + 1) % count, i) for i in range(ends)]),
            ],
            axis=dim,
        )
    return cells


def toeplitz(taps, length, radius):
    index = jnp.arange(length, dtype=jnp.int32)
    offset = index[None, :] - index[:, None] + radius
    count = taps.shape[0]
    onehot = (offset[None, :, :] == jnp.arange(count, dtype=jnp.int32)[:, None, None]).astype(
        jnp.float32
    )
    return jnp.sum(onehot * taps[:, None, None], axis=0)


def along_axial(field, matrix):
    flat = field.reshape(-1, field.shape[2])
    out = jnp.dot(flat, matrix, precision=lax.Precision.HIGHEST, preferred_element_type=jnp.float32)
    return out.reshape(field.shape)


def along_second(field, taps, reverse):
    count = taps.shape[0]
    radius = (count - 1) // 2
    length = field.shape[1]
    padded = jnp.pad(field, ((0, 0), (radius, radius), (0, 0)))
    total = jnp.zeros(field.shape, jnp.float32)
    for tap in range(count):
        start = tap if reverse else 2 * radius - tap
        total = total + taps[tap] * padded[:, start : start + length, :]
    return total


def along_first(padded, taps, reverse):
    count = taps.shape[0]
    radius = (count - 1) // 2
    length = padded.shape[0] - 2 * radius
    total = jnp.zeros((length,) + padded.shape[1:], jnp.float32)
    for tap in range(count):
        start = tap if reverse else 2 * radius - tap
        total = total + taps[tap] * padded[start : start + length]
    return total


def spread(piece):
    return lax.all_gather(piece, "view", axis=1, tiled=True)


def local(estimate, images, taps_first, taps_second, taps_axial):
    first = taps_first[0]
    second = taps_second[0]
    axial = taps_axial[0]
    image = images[0]
    radius = (first.shape[0] - 1) // 2
    matrix = toeplitz(axial, estimate.shape[2], (axial.shape[0] - 1) // 2)
    views = lax.axis_size("view")
    own = estimate
    current = spread(estimate)
    for step in range(ITERS):
        inner = along_second(along_axial(current, matrix), second, False)
        blurred = along_first(extended(inner, (("tile", 0),), radius), first, False)
        ratio = image / blurred
        inner = along_second(along_axial(ratio, matrix.T), second, True)
        total = along_first(extended(inner, (("tile", 0),), radius), first, True)
        share = lax.psum_scatter(total, "view", scatter_dimension=1, tiled=True)
        own = own * (share / views)
        if step + 1 < ITERS:
            current = spread(own)
    return own


def solution(mesh):
    in_specs = (
        P("tile", "view", None),
        P("view", "tile", None, None),
        P("view", None),
        P("view", None),
        P("view", None),
    )
    out_specs = P("tile", "view", None)
    return jax.shard_map(local, mesh=mesh, in_specs=in_specs, out_specs=out_specs, check_vma=False)
```

profile of v0, /device:TPU:1, one launch (start us, length us, event | category | flops | bytes accessed | tf_op | source)
XLA Modules:
  0.0 213.5 jit_solution(13432245626318393699)
XLA Ops:
  7.3 1.6 fusion.79
  9.8 28.1 %all-gather.3.cloned.1.call-done = f32[8,256,128]{2,1,0:T(8,128)} async-done(((f32[8,64,128]{2,1,0:T(8,128)}), f32[8,256,128]{2,1,0:T(8,128)}) %all-gather.3.cloned.1.call-update) | async-done | bytes 1048592 | tf_op jit(solution)/shard_map/all_gather | solution.py:66
  37.9 2.3 %convolution_bitcast_fusion = f32[2048,128]{0,1:T(8,128)S(1)} fusion(f32[128,128]{1,0:T(8,128)S(1)} %select_reduce_fusion, f32[2048,128]{1,0:T(8,128)} %bitcast.33), kind=kOutput, calls=%fused_computation | convolution fusion | flops 402653184 | bytes 2162688 | tf_op jit(solution)/shard_map/dot_general | solution.py:38
  40.6 5.3 %multiply_add_fusion.3 = f32[8,256,128]{2,1,0:T(8,128)S(1)} fusion(f32[8,256,128]{2,1,0:T(8,128)S(1)} %bitcast.32, f32[]{:T(128)} %bitcast.11, f32[]{:T(128)} %bitcast.10, f32[]{:T(128)} %bitcast.9, f32[]{:T(128)} %bitcast.8, f32[]{:T(128)} %bitcast.7, f32[]{:T(128)} %bitcast.6, f32[]{:T(128)} %bitcast.1), kind=kLoop, calls=%fused_computation.87 | loop fusion | flops 3407872 | bytes 2097180 | tf_op jit(solution)/shard_map/add | solution.py:50
  45.9 2.7 %collective-permute-start = (f32[2,256,128]{2,1,0:T(8,128)S(1)}, f32[2,256,128]{2,1,0:T(8,128)S(1)}, u32[]{:S(2)}, u32[]{:S(2)}) collective-permute-start(f32[2,256,128]{2,1,0:T(8,128)S(1)} %get-tuple-element.11), channel_id=1, source_target_pairs={{1,0},{2,1},{3,2},{4,3},{5,4},{6,5},{7,6},{9,8},{10,9},{11,10},{12... | collective-permute-start | bytes 786440 | tf_op jit(solution)/shard_map/ppermute | solution.py:19
  48.6 3.0 %collective-permute-start.1 = (f32[2,256,128]{2,1,0:T(8,128)S(1)}, f32[2,256,128]{2,1,0:T(8,128)S(1)}, u32[]{:S(2)}, u32[]{:S(2)}) collective-permute-start(f32[2,256,128]{2,1,0:T(8,128)S(1)} %get-tuple-element.12), channel_id=1, source_target_pairs={{0,1},{1,2},{2,3},{3,4},{4,5},{5,6},{6,7},{8,9},{9,10},{10,11},{11... | collective-permute-start | bytes 786440 | tf_op jit(solution)/shard_map/ppermute | solution.py:17
  52.3 1.4 collective-permute-done
  53.8 1.2 collective-permute-done.1
  54.9 4.4 %fusion.54 = f32[8,256,128]{2,1,0:T(8,128)S(1)} fusion(f32[2,256,128]{2,1,0:T(8,128)S(1)} %collective-permute-done.1, f32[8,256,128]{2,1,0:T(8,128)S(1)} %multiply_add_fusion.3, f32[2,256,128]{2,1,0:T(8,128)S(1)} %collective-permute-done, f32[1,8,256,128]{3,2,1,0:T(8,128)S(1)} %copy-done.3, f32[]{:T(128)} %bitcast.15, f32[]{:T(128)} %bitcast.14, ...), kind=kOutput, calls=%fused_computation.93 | convolution fusion | flops 406323200 | bytes 3735572 | tf_op jit(solution)/shard_map/dot_general | solution.py:38
  59.3 5.3 %multiply_add_fusion.2 = f32[8,256,128]{2,1,0:T(8,128)S(1)} fusion(f32[8,256,128]{2,1,0:T(8,128)S(1)} %fusion.54, f32[]{:T(128)} %bitcast.11, f32[]{:T(128)} %bitcast.10, f32[]{:T(128)} %bitcast.9, f32[]{:T(128)} %bitcast.8, f32[]{:T(128)} %bitcast.7, f32[]{:T(128)} %bitcast.6, f32[]{:T(128)} %bitcast.1), kind=kLoop, calls=%fused_computation.81 | loop fusion | flops 3407872 | bytes 2097180 | tf_op jit(solution)/shard_map/add | solution.py:50
  64.6 4.4 %collective-permute-start.2 = (f32[2,256,128]{2,1,0:T(8,128)S(1)}, f32[2,256,128]{2,1,0:T(8,128)S(1)}, u32[]{:S(2)}, u32[]{:S(2)}) collective-permute-start(f32[2,256,128]{2,1,0:T(8,128)S(1)} %get-tuple-element.9), channel_id=1, source_target_pairs={{0,1},{1,2},{2,3},{3,4},{4,5},{5,6},{6,7},{8,9},{9,10},{10,11},{11... | collective-permute-start | bytes 786440 | tf_op jit(solution)/shard_map/ppermute | solution.py:17
  69.0 1.9 collective-permute-start.3
  71.0 1.4 collective-permute-done.2
  72.3 4.4 %collective-permute-done.3 = f32[2,256,128]{2,1,0:T(8,128)S(1)} collective-permute-done((f32[2,256,128]{2,1,0:T(8,128)S(1)}, f32[2,256,128]{2,1,0:T(8,128)S(1)}, u32[]{:S(2)}, u32[]{:S(2)}) %collective-permute-start.3) | collective-permute-done | bytes 262176 | tf_op jit(solution)/shard_map/ppermute | solution.py:19
  76.7 4.4 %fusion.20 = f32[8,256,128]{2,1,0:T(8,128)} fusion(f32[8,256,128]{2,1,0:T(8,128)S(1)} %multiply_add_fusion.2, f32[2,256,128]{2,1,0:T(8,128)S(1)} %collective-permute-done.3, f32[2,256,128]{2,1,0:T(8,128)S(1)} %collective-permute-done.2, f32[]{:T(128)} %bitcast.15, f32[]{:T(128)} %bitcast.14, f32[]{:T(128)} %bitcast.13, f32[]{:T(128)} %bitcast.12, f32[]{:T(128)} %bitcast), kind=kLoop, calls=%fused_computation.39 | loop fusion | flops 3407872 | bytes 2621460 | tf_op jit(solution)/shard_map/add | solution.py:61
  81.2 26.4 %reduce-scatter.3.cloned.1.call-done = f32[8,64,128]{2,1,0:T(8,128)} async-done(((f32[8,256,128]{2,1,0:T(8,128)}), f32[8,64,128]{2,1,0:T(8,128)}) %reduce-scatter.3.cloned.1.call-update) | async-done | bytes 262160 | tf_op jit(solution)/shard_map/reduce_scatter | solution.py:85
  107.6 1.7 multiply_multiply_fusion.1
  109.4 26.9 %all-gather.5.cloned.1.call-done = f32[8,256,128]{2,1,0:T(8,128)} async-done(((f32[8,64,128]{2,1,0:T(8,128)}), f32[8,256,128]{2,1,0:T(8,128)}) %all-gather.5.cloned.1.call-update) | async-done | bytes 1048592 | tf_op jit(solution)/shard_map/all_gather | solution.py:66
  136.3 2.2 %fusion.69 = f32[8,256,128]{2,1,0:T(8,128)S(1)} fusion(f32[8,256,128]{2,1,0:T(8,128)} %all-gather.5.cloned.1.call-done, f32[128,128]{1,0:T(8,128)S(1)} %select_reduce_fusion), kind=kOutput, calls=%fused_computation.108 | convolution fusion | flops 402653184 | bytes 2162688 | tf_op jit(solution)/shard_map/dot_general | solution.py:38
  138.5 5.3 %multiply_add_fusion.1 = f32[8,256,128]{2,1,0:T(8,128)S(1)} fusion(f32[8,256,128]{2,1,0:T(8,128)S(1)} %fusion.69, f32[]{:T(128)} %bitcast.11, f32[]{:T(128)} %bitcast.10, f32[]{:T(128)} %bitcast.9, f32[]{:T(128)} %bitcast.8, f32[]{:T(128)} %bitcast.7, f32[]{:T(128)} %bitcast.6, f32[]{:T(128)} %bitcast.1), kind=kLoop, calls=%fused_computation.75 | loop fusion | flops 3407872 | bytes 2097180 | tf_op jit(solution)/shard_map/add | solution.py:50
  143.8 2.6 %collective-permute-start.4 = (f32[2,256,128]{2,1,0:T(8,128)S(1)}, f32[2,256,128]{2,1,0:T(8,128)S(1)}, u32[]{:S(2)}, u32[]{:S(2)}) collective-permute-start(f32[2,256,128]{2,1,0:T(8,128)S(1)} %get-tuple-element.7), channel_id=1, source_target_pairs={{1,0},{2,1},{3,2},{4,3},{5,4},{6,5},{7,6},{9,8},{10,9},{11,10},{12... | collective-permute-start | bytes 786440 | tf_op jit(solution)/shard_map/ppermute | solution.py:19
  146.4 3.0 %collective-permute-start.5 = (f32[2,256,128]{2,1,0:T(8,128)S(1)}, f32[2,256,128]{2,1,0:T(8,128)S(1)}, u32[]{:S(2)}, u32[]{:S(2)}) collective-permute-start(f32[2,256,128]{2,1,0:T(8,128)S(1)} %get-tuple-element.8), channel_id=1, source_target_pairs={{0,1},{1,2},{2,3},{3,4},{4,5},{5,6},{6,7},{8,9},{9,10},{10,11},{11... | collective-permute-start | bytes 786440 | tf_op jit(solution)/shard_map/ppermute | solution.py:17
  149.4 2.1 collective-permute-done.4
  152.7 4.4 %fusion.56 = f32[8,256,128]{2,1,0:T(8,128)S(1)} fusion(f32[2,256,128]{2,1,0:T(8,128)S(1)} %collective-permute-done.5, f32[8,256,128]{2,1,0:T(8,128)S(1)} %multiply_add_fusion.1, f32[2,256,128]{2,1,0:T(8,128)S(1)} %collective-permute-done.4, f32[1,8,256,128]{3,2,1,0:T(8,128)S(1)} %copy-done.3, f32[]{:T(128)} %bitcast.15, f32[]{:T(128)} %bitcast.14, ...), kind=kOutput, calls=%fused_computation.94 | convolution fusion | flops 406323200 | bytes 3735572 | tf_op jit(solution)/shard_map/dot_general | solution.py:38
  157.1 5.3 %multiply_add_fusion = f32[8,256,128]{2,1,0:T(8,128)S(1)} fusion(f32[8,256,128]{2,1,0:T(8,128)S(1)} %fusion.56, f32[]{:T(128)} %bitcast.11, f32[]{:T(128)} %bitcast.10, f32[]{:T(128)} %bitcast.9, f32[]{:T(128)} %bitcast.8, f32[]{:T(128)} %bitcast.7, f32[]{:T(128)} %bitcast.6, f32[]{:T(128)} %bitcast.1), kind=kLoop, calls=%fused_computation.69 | loop fusion | flops 3407872 | bytes 2097180 | tf_op jit(solution)/shard_map/add | solution.py:50
  162.4 4.4 %collective-permute-start.6 = (f32[2,256,128]{2,1,0:T(8,128)S(1)}, f32[2,256,128]{2,1,0:T(8,128)S(1)}, u32[]{:S(2)}, u32[]{:S(2)}) collective-permute-start(f32[2,256,128]{2,1,0:T(8,128)S(1)} %get-tuple-element.5), channel_id=1, source_target_pairs={{0,1},{1,2},{2,3},{3,4},{4,5},{5,6},{6,7},{8,9},{9,10},{10,11},{11... | collective-permute-start | bytes 786440 | tf_op jit(solution)/shard_map/ppermute | solution.py:17
  166.8 1.9 collective-permute-start.7
  168.7 1.4 collective-permute-done.6
  170.1 4.4 %collective-permute-done.7 = f32[2,256,128]{2,1,0:T(8,128)S(1)} collective-permute-done((f32[2,256,128]{2,1,0:T(8,128)S(1)}, f32[2,256,128]{2,1,0:T(8,128)S(1)}, u32[]{:S(2)}, u32[]{:S(2)}) %collective-permute-start.7) | collective-permute-done | bytes 262176 | tf_op jit(solution)/shard_map/ppermute | solution.py:19
  174.5 4.4 %fusion.3 = f32[8,256,128]{2,1,0:T(8,128)} fusion(f32[8,256,128]{2,1,0:T(8,128)S(1)} %multiply_add_fusion, f32[2,256,128]{2,1,0:T(8,128)S(1)} %collective-permute-done.7, f32[2,256,128]{2,1,0:T(8,128)S(1)} %collective-permute-done.6, f32[]{:T(128)} %bitcast.15, f32[]{:T(128)} %bitcast.14, f32[]{:T(128)} %bitcast.13, f32[]{:T(128)} %bitcast.12, f32[]{:T(128)} %bitcast), kind=kLoop, calls=%fused_computation.22 | loop fusion | flops 3407872 | bytes 2621460 | tf_op jit(solution)/shard_map/add | solution.py:61
  178.9 26.4 %reduce-scatter.5.cloned.1.call-done = f32[8,64,128]{2,1,0:T(8,128)} async-done(((f32[8,256,128]{2,1,0:T(8,128)}), f32[8,64,128]{2,1,0:T(8,128)}) %reduce-scatter.5.cloned.1.call-update) | async-done | bytes 262160 | tf_op jit(solution)/shard_map/reduce_scatter | solution.py:85
  205.3 1.7 multiply_multiply_fusion
  (25 shorter events, 4.2 us)
Async XLA Ops:
  6.5 31.4 %all-gather.3.cloned.1.call-start = ((), (), s32[]{:S(2)}) async-start(), calls=%async_computation.2 | async-start | bytes 1310720 | tf_op jit(solution)/shard_map/all_gather | solution.py:66
  7.3 100.3 %reduce-scatter.3.cloned.1.call-start = ((), (), s32[]{:S(2)}) async-start(), calls=%async_computation.3 | async-start | bytes 1310720 | tf_op jit(solution)/shard_map/reduce_scatter | solution.py:85
  45.8 5.8 %copy-start.2 = (f32[1,5]{1,0:T(1,128)S(1)}, f32[1,5]{1,0:T(1,128)}, u32[]{:S(2)}) copy-start(f32[1,5]{1,0:T(1,128)} %param.7) | copy-start | bytes 64
  45.8 9.1 %copy-start.3 = (f32[1,8,256,128]{3,2,1,0:T(8,128)S(1)}, f32[1,8,256,128]{3,2,1,0:T(8,128)}, u32[]{:S(2)}) copy-start(f32[1,8,256,128]{3,2,1,0:T(8,128)} %param.6) | copy-start | bytes 3145732
  45.9 7.9 %collective-permute-start = (f32[2,256,128]{2,1,0:T(8,128)S(1)}, f32[2,256,128]{2,1,0:T(8,128)S(1)}, u32[]{:S(2)}, u32[]{:S(2)}) collective-permute-start(f32[2,256,128]{2,1,0:T(8,128)S(1)} %get-tuple-element.11), channel_id=1, source_target_pairs={{1,0},{2,1},{3,2},{4,3},{5,4},{6,5},{7,6},{9,8},{10,9},{11,10},{12... | collective-permute-start | bytes 786440 | tf_op jit(solution)/shard_map/ppermute | solution.py:19
  48.6 6.3 %collective-permute-start.1 = (f32[2,256,128]{2,1,0:T(8,128)S(1)}, f32[2,256,128]{2,1,0:T(8,128)S(1)}, u32[]{:S(2)}, u32[]{:S(2)}) collective-permute-start(f32[2,256,128]{2,1,0:T(8,128)S(1)} %get-tuple-element.12), channel_id=1, source_target_pairs={{0,1},{1,2},{2,3},{3,4},{4,5},{5,6},{6,7},{8,9},{9,10},{10,11},{11... | collective-permute-start | bytes 786440 | tf_op jit(solution)/shard_map/ppermute | solution.py:17
  64.6 7.7 %collective-permute-start.2 = (f32[2,256,128]{2,1,0:T(8,128)S(1)}, f32[2,256,128]{2,1,0:T(8,128)S(1)}, u32[]{:S(2)}, u32[]{:S(2)}) collective-permute-start(f32[2,256,128]{2,1,0:T(8,128)S(1)} %get-tuple-element.9), channel_id=1, source_target_pairs={{0,1},{1,2},{2,3},{3,4},{4,5},{5,6},{6,7},{8,9},{9,10},{10,11},{11... | collective-permute-start | bytes 786440 | tf_op jit(solution)/shard_map/ppermute | solution.py:17
  69.0 7.7 %collective-permute-start.3 = (f32[2,256,128]{2,1,0:T(8,128)S(1)}, f32[2,256,128]{2,1,0:T(8,128)S(1)}, u32[]{:S(2)}, u32[]{:S(2)}) collective-permute-start(f32[2,256,128]{2,1,0:T(8,128)S(1)} %get-tuple-element.10), channel_id=1, source_target_pairs={{1,0},{2,1},{3,2},{4,3},{5,4},{6,5},{7,6},{9,8},{10,9},{11,10},{12... | collective-permute-start | bytes 786440 | tf_op jit(solution)/shard_map/ppermute | solution.py:19
  81.1 26.5 %copy-start.1 = (f32[8,64,128]{2,1,0:T(8,128)S(1)}, f32[8,64,128]{2,1,0:T(8,128)}, u32[]{:S(2)}) copy-start(f32[8,64,128]{2,1,0:T(8,128)} %param.5) | copy-start | bytes 786436
  81.2 55.1 %all-gather.5.cloned.1.call-start = ((), (), s32[]{:S(2)}) async-start(), calls=%async_computation.4 | async-start | bytes 1310720 | tf_op jit(solution)/shard_map/all_gather | solution.py:66
  109.3 96.0 %reduce-scatter.5.cloned.1.call-start = ((), (), s32[]{:S(2)}) async-start(), calls=%async_computation.5 | async-start | bytes 1310720 | tf_op jit(solution)/shard_map/reduce_scatter | solution.py:85
  143.8 7.7 %collective-permute-start.4 = (f32[2,256,128]{2,1,0:T(8,128)S(1)}, f32[2,256,128]{2,1,0:T(8,128)S(1)}, u32[]{:S(2)}, u32[]{:S(2)}) collective-permute-start(f32[2,256,128]{2,1,0:T(8,128)S(1)} %get-tuple-element.7), channel_id=1, source_target_pairs={{1,0},{2,1},{3,2},{4,3},{5,4},{6,5},{7,6},{9,8},{10,9},{11,10},{12... | collective-permute-start | bytes 786440 | tf_op jit(solution)/shard_map/ppermute | solution.py:19
  146.4 6.3 %collective-permute-start.5 = (f32[2,256,128]{2,1,0:T(8,128)S(1)}, f32[2,256,128]{2,1,0:T(8,128)S(1)}, u32[]{:S(2)}, u32[]{:S(2)}) collective-permute-start(f32[2,256,128]{2,1,0:T(8,128)S(1)} %get-tuple-element.8), channel_id=1, source_target_pairs={{0,1},{1,2},{2,3},{3,4},{4,5},{5,6},{6,7},{8,9},{9,10},{10,11},{11... | collective-permute-start | bytes 786440 | tf_op jit(solution)/shard_map/ppermute | solution.py:17
  162.4 7.7 %collective-permute-start.6 = (f32[2,256,128]{2,1,0:T(8,128)S(1)}, f32[2,256,128]{2,1,0:T(8,128)S(1)}, u32[]{:S(2)}, u32[]{:S(2)}) collective-permute-start(f32[2,256,128]{2,1,0:T(8,128)S(1)} %get-tuple-element.5), channel_id=1, source_target_pairs={{0,1},{1,2},{2,3},{3,4},{4,5},{5,6},{6,7},{8,9},{9,10},{10,11},{11... | collective-permute-start | bytes 786440 | tf_op jit(solution)/shard_map/ppermute | solution.py:17
  166.8 7.7 %collective-permute-start.7 = (f32[2,256,128]{2,1,0:T(8,128)S(1)}, f32[2,256,128]{2,1,0:T(8,128)S(1)}, u32[]{:S(2)}, u32[]{:S(2)}) collective-permute-start(f32[2,256,128]{2,1,0:T(8,128)S(1)} %get-tuple-element.6), channel_id=1, source_target_pairs={{1,0},{2,1},{3,2},{4,3},{5,4},{6,5},{7,6},{9,8},{10,9},{11,10},{12... | collective-permute-start | bytes 786440 | tf_op jit(solution)/shard_map/ppermute | solution.py:19
  178.9 26.5 %copy-start = (f32[8,64,128]{2,1,0:T(8,128)S(1)}, f32[8,64,128]{2,1,0:T(8,128)}, u32[]{:S(2)}) copy-start(f32[8,64,128]{2,1,0:T(8,128)} %multiply_multiply_fusion.1) | copy-start | bytes 786436
Sparse Core Ops, SparseCore 0:
  9.2 28.6 all-gather.2
  81.3 26.2 reduce-scatter.2
  109.6 26.6 all-gather.4
  179.0 26.2 reduce-scatter.4
where the time goes:
time: 215 us; the launch traced here: 214 us
  waiting for transfers between devices  126 us (59%)
  other arithmetic  34.2 us (16%)
  starting transfers between devices  24.1 us (11%)
  between operations  13.3 us (6%)
  matrix products  13.2 us (6%)
  local copies, waits for them, and re-layouts  2.74 us (1%)
    all_gather x2, waiting for transfers between devices, spread(): return lax.all_gather(piece, 'view', axis=1, tiled=True)  55 us
    reduce_scatter x2, waiting for transfers between devices, local(): share = lax.psum_scatter(total, 'view', scatter_dimension=1, tiled=True)  52.8 us
    add x4, other arithmetic, along_second(): total = total + taps[tap] * padded[:, start:start + length, :]  21 us
    ppermute x4, starting transfers between devices, extended(): lax.ppermute(tail, axis, [(i, (i + 1) % count) for i in range(ends)])  14.8 us
    dot_general x4, matrix products, along_axial(): jnp.dot(flat, matrix, precision=lax.Precision.HIGHEST, preferred_element_...  13.2 us
    ppermute x4, waiting for transfers between devices, extended(): lax.ppermute(head, axis, [((i + 1) % count, i) for i in range(ends)])  12.3 us
    ppermute x4, starting transfers between devices, extended(): lax.ppermute(head, axis, [((i + 1) % count, i) for i in range(ends)])  9.14 us
    add x2, other arithmetic, along_first(): total = total + taps[tap] * padded[start:start + length]  8.85 us
  transfers between devices with their start and end apart: 12, of which 12 were waited for; matrix products, arithmetic and copies ran while one was open for 1% of the time, Pallas kernels for 0%

commit v1 on v0

v1 whole, which is shorter than its diff:
```python
import functools

import jax
import jax.numpy as jnp
from jax import lax
from jax.experimental import pallas as pl
from jax.experimental.pallas import tpu as pltpu
from jax.sharding import PartitionSpec as P

ITERS = 2
PAD = 8
DIRECTIONS = [(0, -1), (0, 1), (-1, -1), (-1, 1), (1, -1), (1, 1), (-1, 0), (1, 0)]
MESH_ID = pl.DeviceIdType.MESH


def split(x):
    hi = x.astype(jnp.bfloat16)
    lo = (x - hi.astype(jnp.float32)).astype(jnp.bfloat16)
    return hi, lo


def kernel(
    views, tiles, rf, rs, ra,
    est_ref, img_ref, tf_ref, ts_ref, ta_ref, out_ref,
    est, ext, planes, bplane, rplane, gplanes, left, left2, wconv, wcorr, pack, img, over,
    img_send, img_recv, pk_send, pk_recv, local_sem, h_send, h_recv, o_send, o_recv,
):
    nx, ny, nz = est_ref.shape
    nf, ns, na = 2 * rf + 1, 2 * rs + 1, 2 * ra + 1
    frame = ny + 2 * PAD
    full = nx + 2 * rf
    v = lax.axis_index("view")
    t = lax.axis_index("tile")
    mid = pl.ds(PAD, ny)
    f32 = jnp.float32

    def inside(dt, dv):
        ok = None
        for d, at, count in ((dt, t, tiles), (dv, v, views)):
            if d:
                here = at + d < count if d > 0 else at + d >= 0
                ok = here if ok is None else jnp.logical_and(ok, here)
        return ok

    own = pltpu.make_async_copy(
        img_ref.at[0, :, pl.ds(pl.multiple_of(v * ny, 8), ny), :], img.at[v], local_sem
    )
    own.start()

    for it in range(ITERS):
        est[it] = jnp.zeros(est.shape[1:], f32)
    est[0, rf : rf + nx, mid, :] = est_ref[...]
    pack[v] = jnp.zeros(pack.shape[1:], f32)
    for k in range(nf):
        pack[v, k : k + 1, :] = jnp.broadcast_to(tf_ref[0:1, k : k + 1], (1, nz))
    for k in range(ns):
        pack[v, nf + k : nf + k + 1, :] = jnp.broadcast_to(ts_ref[0:1, k : k + 1], (1, nz))
    pack[v, nf + ns : nf + ns + 1, 0:na] = ta_ref[...]

    barrier = pltpu.get_barrier_semaphore()
    for d in range(1, views):
        peer = lax.rem(v + d, views)
        pl.semaphore_signal(barrier, inc=1, device_id=(peer, t), device_id_type=MESH_ID)
    for dt, dv in DIRECTIONS:
        if dt:
            @pl.when(inside(dt, dv))
            def _(dt=dt, dv=dv):
                pl.semaphore_signal(
                    barrier, inc=1, device_id=(v + dv, t + dt), device_id_type=MESH_ID
                )
    sides = jnp.where(t > 0, 1, 0) + jnp.where(t < tiles - 1, 1, 0)
    rows = 1 + jnp.where(v > 0, 1, 0) + jnp.where(v < views - 1, 1, 0)
    pl.semaphore_wait(barrier, views - 1 + sides * rows)

    def halo(it, n):
        dt, dv = DIRECTIONS[n]
        sp, dp, cp = {0: (rf, rf, nx), 1: (nx, 0, rf), -1: (rf, rf + nx, rf)}[dt]
        sr, dr, cr = {0: (PAD, PAD, ny), 1: (ny, 0, PAD), -1: (PAD, PAD + ny, PAD)}[dv]
        return pltpu.make_async_remote_copy(
            src_ref=est.at[it, pl.ds(sp, cp), pl.ds(sr, cr), :],
            dst_ref=est.at[it, pl.ds(dp, cp), pl.ds(dr, cr), :],
            send_sem=h_send.at[it, n], recv_sem=h_recv.at[it, n],
            device_id=(v + dv, t + dt), device_id_type=MESH_ID,
        )

    def region(n):
        dt, dv = DIRECTIONS[n]
        sp, dp, cp = {0: (rf, rf, nx), 1: (rf + nx, rf, rf), -1: (0, nx, rf)}[dt]
        sr, dr, cr = {0: (PAD, PAD, ny), 1: (PAD + ny, PAD, PAD), -1: (0, ny, PAD)}[dv]
        return sp, dp, cp, sr, dr, cr

    def overhang(it, n):
        dt, dv = DIRECTIONS[n]
        sp, dp, cp, sr, dr, cr = region(n)
        return pltpu.make_async_remote_copy(
            src_ref=ext.at[it, pl.ds(sp, cp), pl.ds(sr, cr), :],
            dst_ref=over.at[it, n, pl.ds(0, cp), pl.ds(0, cr), :],
            send_sem=o_send.at[it, n], recv_sem=o_recv.at[it, n],
            device_id=(v + dv, t + dt), device_id_type=MESH_ID,
        )

    def each(make, it, method, sending):
        for n, (dt, dv) in enumerate(DIRECTIONS):
            sign = 1 if sending else -1

            @pl.when(inside(sign * dt, sign * dv))
            def _(n=n):
                getattr(make(it, n), method)()

    def send_pack(d):
        peer = lax.rem(v + d, views)
        return pltpu.make_async_remote_copy(
            src_ref=pack.at[v], dst_ref=pack.at[v],
            send_sem=pk_send.at[d], recv_sem=pk_recv.at[views - d],
            device_id=(peer, t), device_id_type=MESH_ID,
        )

    def send_img(d):
        peer = lax.rem(v + d, views)
        return pltpu.make_async_remote_copy(
            src_ref=img_ref.at[0, :, pl.ds(pl.multiple_of(peer * ny, 8), ny), :],
            dst_ref=img.at[v],
            send_sem=img_send.at[d], recv_sem=img_recv.at[views - d],
            device_id=(peer, t), device_id_type=MESH_ID,
        )

    def arrived(buffer, sem, s, w):
        peer = lax.rem(v + s, views)
        pltpu.make_async_remote_copy(
            src_ref=buffer.at[w], dst_ref=buffer.at[w],
            send_sem=sem.at[s], recv_sem=sem.at[s],
            device_id=(peer, t), device_id_type=MESH_ID,
        ).wait_recv()

    each(halo, 0, "start", True)
    for d in range(1, views):
        send_pack(d).start()
    for d in range(1, views):
        send_img(d).start()

    rplane[...] = jnp.zeros(rplane.shape, f32)

    for it in range(ITERS):
        each(halo, it, "wait_recv", False)
        hi, lo = split(est[it].reshape(full * frame, nz))
        left[:, 0:nz] = hi
        left[:, nz : 2 * nz] = lo
        left[:, 2 * nz : 3 * nz] = hi

        def view(s, carry):
            w = lax.rem(v + s, views)
            if it == 0:
                @pl.when(s > 0)
                def _():
                    arrived(pack, pk_recv, s, w)

                row = jnp.broadcast_to(pack[w, nf + ns : nf + ns + 1, :], (nz, nz))
                i = lax.broadcasted_iota(jnp.int32, (nz, nz), 0)
                j = lax.broadcasted_iota(jnp.int32, (nz, nz), 1)
                matrix = pltpu.roll(row, nz - ra, axis=1, stride=1, stride_axis=0)
                matrix = jnp.where(jnp.abs(i - j) <= ra, matrix, 0.0)
                for ref, m in ((wconv, matrix), (wcorr, matrix.T)):
                    hi, lo = split(m)
                    ref[w, 0:nz, :] = hi
                    ref[w, nz : 2 * nz, :] = hi
                    ref[w, 2 * nz : 3 * nz, :] = lo

            planes[...] = jnp.dot(
                left[...], wconv[w], preferred_element_type=f32
            ).reshape(full, frame, nz)
            first = [pack[w, k : k + 1, :] for k in range(nf)]
            second = [pack[w, nf + k : nf + k + 1, :] for k in range(ns)]
            if it == 0:
                @pl.when(s > 0)
                def _():
                    arrived(img, img_recv, s, w)

                @pl.when(s == 0)
                def _():
                    own.wait()

            for x in range(nx):
                bplane[x] = sum(first[k] * planes[x + nf - 1 - k] for k in range(nf))
                blurred = sum(
                    second[k] * bplane[x, pl.ds(PAD + rs - k, ny), :] for k in range(ns)
                )
                rplane[x, pl.ds(2 * PAD, ny), :] = img[w, x] / blurred
                gplanes[x] = sum(
                    second[k] * rplane[x, pl.ds(PAD - rs + k, frame), :] for k in range(ns)
                )
            for x in range(full):
                total = sum(
                    first[k] * gplanes[x + k - (nf - 1)]
                    for k in range(nf)
                    if 0 <= x + k - (nf - 1) < nx
                )
                hi, lo = split(total)
                rows = pl.ds(x * frame, frame)
                left2[rows, 0:nz] = hi
                left2[rows, nz : 2 * nz] = lo
                left2[rows, 2 * nz : 3 * nz] = hi
            part = jnp.dot(left2[...], wcorr[w], preferred_element_type=f32).reshape(
                full, frame, nz
            )

            @pl.when(s == 0)
            def _():
                ext[it] = part

            @pl.when(s > 0)
            def _():
                ext[it] = ext[it] + part

            return carry

        lax.fori_loop(0, views, view, 0)
        each(overhang, it, "start", True)
        for n, (dt, dv) in enumerate(DIRECTIONS):
            @pl.when(inside(-dt, -dv))
            def _(n=n):
                overhang(it, n).wait_recv()
                _, dp, cp, _, dr, cr = region(n)
                place = (it, pl.ds(dp, cp), pl.ds(dr, cr), slice(None))
                ext[place] = ext[place] + over[it, n, pl.ds(0, cp), pl.ds(0, cr), :]

        for x in range(nx):
            new = est[it, rf + x, mid, :] * (ext[it, rf + x, mid, :] / views)
            if it + 1 < ITERS:
                est[it + 1, rf + x, mid, :] = new
            else:
                out_ref[x] = new
        if it + 1 < ITERS:
            each(halo, it + 1, "start", True)

    for it in range(ITERS):
        each(halo, it, "wait_send", True)
        each(overhang, it, "wait_send", True)
    for d in range(1, views):
        send_pack(d).wait_send()
        send_img(d).wait_send()


def local(views, tiles, estimate, images, taps_first, taps_second, taps_axial):
    nx, ny, nz = estimate.shape
    rf, rs, ra = [(taps.shape[1] - 1) // 2 for taps in (taps_first, taps_second, taps_axial)]
    frame = ny + 2 * PAD
    full = nx + 2 * rf
    f32, bf16 = jnp.float32, jnp.bfloat16
    vmem = pl.BlockSpec(memory_space=pltpu.VMEM)
    dma = pltpu.SemaphoreType.DMA
    directions = len(DIRECTIONS)
    rows = -(-(2 * rf + 2 * rs + 3) // 8) * 8
    return pl.pallas_call(
        functools.partial(kernel, views, tiles, rf, rs, ra),
        out_shape=jax.ShapeDtypeStruct(estimate.shape, f32),
        in_specs=[vmem, pl.BlockSpec(memory_space=pl.ANY), vmem, vmem, vmem],
        out_specs=vmem,
        scratch_shapes=[
            pltpu.VMEM((ITERS, full, frame, nz), f32),
            pltpu.VMEM((ITERS, full, frame, nz), f32),
            pltpu.VMEM((full, frame, nz), f32),
            pltpu.VMEM((nx, frame, nz), f32),
            pltpu.VMEM((nx, frame + 2 * PAD, nz), f32),
            pltpu.VMEM((nx, frame, nz), f32),
            pltpu.VMEM((full * frame, 3 * nz), bf16),
            pltpu.VMEM((full * frame, 3 * nz), bf16),
            pltpu.VMEM((views, 3 * nz, nz), bf16),
            pltpu.VMEM((views, 3 * nz, nz), bf16),
            pltpu.VMEM((views, rows, nz), f32),
            pltpu.VMEM((views, nx, ny, nz), f32),
            pltpu.VMEM((ITERS, directions, nx, ny, nz), f32),
            dma((views,)), dma((views,)), dma((views,)), dma((views,)), dma,
            dma((ITERS, directions)), dma((ITERS, directions)),
            dma((ITERS, directions)), dma((ITERS, directions)),
        ],
        compiler_params=pltpu.CompilerParams(
            collective_id=0, has_side_effects=True, vmem_limit_bytes=40 * 2**20
        ),
    )(estimate, images, taps_first, taps_second, taps_axial)


def solution(mesh):
    in_specs = (
        P("tile", "view", None),
        P("view", "tile", None, None),
        P("view", None),
        P("view", None),
        P("view", None),
    )
    out_specs = P("tile", "view", None)
    call = functools.partial(local, mesh.shape["view"], mesh.shape["tile"])
    return jax.shard_map(call, mesh=mesh, in_specs=in_specs, out_specs=out_specs, check_vma=False)
```

time: 215 us -> 46 us (0.21)
  waiting for transfers between devices: 126 us -> 0 us
  Pallas kernels: 0 us -> 40.8 us
  other arithmetic: 34.2 us -> 0 us
  starting transfers between devices: 24.1 us -> 0 us
  between operations: 13.3 us -> 0.01 us
  matrix products: 13.2 us -> 0 us
    all_gather x2 -> x0, waiting for transfers between devices: 55 us -> none  [spread(): return lax.all_gather(piece, 'view', axis=1, tiled=True)]
    reduce_scatter x2 -> x0, waiting for transfers between devices: 52.8 us -> none  [local(): share = lax.psum_scatter(total, 'view', scatter_dimension=1, tiled=True)]
    pallas_call x0 -> x1, Pallas kernels: none -> 40.8 us  [local(): pl.pallas_call(functools.partial(kernel, views, tiles, rf, rs, ra), out_s...]
    add x7 -> x0, other arithmetic: 29.9 us -> none  [the longest x4 21 us: along_second(): total = total + taps[tap] * padded[:, start:start + length, :]]
    ppermute x8 -> x0, starting transfers between devices: 23.9 us -> none  [the longest x4 14.8 us: extended(): lax.ppermute(tail, axis, [(i, (i + 1) % count) for i in range(ends)])]
    ppermute x8 -> x0, waiting for transfers between devices: 17.4 us -> none  [the longest x4 12.3 us: extended(): lax.ppermute(head, axis, [((i + 1) % count, i) for i in range(ends)])]
    dot_general x4 -> x0, matrix products: 13.2 us -> none  [along_axial(): jnp.dot(flat, matrix, precision=lax.Precision.HIGHEST, preferred_element_...]
    unnamed x8 -> x11, local copies, waits for them, and re-layouts: 0.02 us -> 4.84 us
  transfers between devices with their start and end apart: 12 -> 0, of which waited for: 12 -> 0; matrix products, arithmetic and copies ran while one was open for 1% -> 0% of each run, Pallas kernels for 0% -> 0%
where the time goes in v1:
time: 46 us; the launch traced here: 45.6 us
  Pallas kernels  40.8 us (89%)
  local copies, waits for them, and re-layouts  4.84 us (11%)
    pallas_call x1, Pallas kernels, local(): pl.pallas_call(functools.partial(kernel, views, tiles, rf, rs, ra), out_s...  40.8 us
    unnamed x11, local copies, waits for them, and re-layouts  4.84 us

profile of v1, /device:TPU:1, one launch (start us, length us, event | category | flops | bytes accessed | tf_op | source)
XLA Modules:
  0.0 45.6 jit_solution(7657198829718553944)
XLA Ops:
  0.0 0.0 copy-start
  0.0 1.2 %copy-done = f32[1,8,256,128]{3,2,1,0:T(8,128)S(1)} copy-done((f32[1,8,256,128]{3,2,1,0:T(8,128)S(1)}, f32[1,8,256,128]{3,2,1,0:T(8,128)}, u32[]{:S(2)}) %copy-start) | copy-done | bytes 1048600
  1.2 0.0 copy-start.1
  1.2 0.9 %copy-done.1 = f32[8,64,128]{2,1,0:T(8,128)S(1)} copy-done((f32[8,64,128]{2,1,0:T(8,128)S(1)}, f32[8,64,128]{2,1,0:T(8,128)}, u32[]{:S(2)}) %copy-start.1) | copy-done | bytes 262168
  2.2 0.0 copy-start.2
  2.2 0.7 %copy-done.2 = f32[1,5]{1,0:T(1,128)S(1)} copy-done((f32[1,5]{1,0:T(1,128)S(1)}, f32[1,5]{1,0:T(1,128)}, u32[]{:S(2)}) %copy-start.2) | copy-done | bytes 44
  2.8 0.0 copy-start.3
  2.8 0.7 %copy-done.3 = f32[1,7]{1,0:T(1,128)S(1)} copy-done((f32[1,7]{1,0:T(1,128)S(1)}, f32[1,7]{1,0:T(1,128)}, u32[]{:S(2)}) %copy-start.3) | copy-done | bytes 52
  3.5 0.0 copy-start.4
  3.5 0.7 %copy-done.4 = f32[1,33]{1,0:T(1,128)S(1)} copy-done((f32[1,33]{1,0:T(1,128)S(1)}, f32[1,33]{1,0:T(1,128)}, u32[]{:S(2)}) %copy-start.4) | copy-done | bytes 156
  4.1 40.8 %shard_map.55 = f32[8,64,128]{2,1,0:T(8,128)S(1)} custom-call(f32[8,64,128]{2,1,0:T(8,128)S(1)} %copy-done.1, f32[1,8,256,128]{3,2,1,0:T(8,128)S(1)} %copy-done, f32[1,5]{1,0:T(1,128)S(1)} %copy-done.2, f32[1,7]{1,0:T(1,128)S(1)} %copy-done.3, f32[1,33]{1,0:T(1,128)S(1)} %copy-done.4), custom_call_target="tpu_custom_call" | custom-call | tf_op jit(solution)/shard_map/pallas_call | solution.py:253
  44.9 0.7 %copy.7 = f32[8,64,128]{2,1,0:T(8,128)} copy(f32[8,64,128]{2,1,0:T(8,128)S(1)} %shard_map.55) | data formatting | bytes 524288
Async XLA Ops:
  0.0 1.2 %copy-start = (f32[1,8,256,128]{3,2,1,0:T(8,128)S(1)}, f32[1,8,256,128]{3,2,1,0:T(8,128)}, u32[]{:S(2)}) copy-start(f32[1,8,256,128]{3,2,1,0:T(8,128)} %img_ref.1) | copy-start | bytes 3145732
  1.2 0.9 %copy-start.1 = (f32[8,64,128]{2,1,0:T(8,128)S(1)}, f32[8,64,128]{2,1,0:T(8,128)}, u32[]{:S(2)}) copy-start(f32[8,64,128]{2,1,0:T(8,128)} %est_ref.1) | copy-start | bytes 786436
  2.2 0.7 %copy-start.2 = (f32[1,5]{1,0:T(1,128)S(1)}, f32[1,5]{1,0:T(1,128)}, u32[]{:S(2)}) copy-start(f32[1,5]{1,0:T(1,128)} %tf_ref.1) | copy-start | bytes 64
  2.8 0.7 %copy-start.3 = (f32[1,7]{1,0:T(1,128)S(1)}, f32[1,7]{1,0:T(1,128)}, u32[]{:S(2)}) copy-start(f32[1,7]{1,0:T(1,128)} %ts_ref.1) | copy-start | bytes 88
  3.5 0.7 %copy-start.4 = (f32[1,33]{1,0:T(1,128)S(1)}, f32[1,33]{1,0:T(1,128)}, u32[]{:S(2)}) copy-start(f32[1,33]{1,0:T(1,128)} %ta_ref.1) | copy-start | bytes 400

commit v2 on v1

v2 whole, which is shorter than its diff:
```python
import functools

import jax
import jax.numpy as jnp
from jax import lax
from jax.experimental import pallas as pl
from jax.experimental.pallas import tpu as pltpu
from jax.sharding import PartitionSpec as P

ITERS = 2
PAD = 8
DIRECTIONS = [(0, -1), (0, 1), (-1, -1), (-1, 1), (1, -1), (1, 1), (-1, 0), (1, 0)]
MESH_ID = pl.DeviceIdType.MESH


def split(x):
    hi = x.astype(jnp.bfloat16)
    lo = (x - hi.astype(jnp.float32)).astype(jnp.bfloat16)
    return hi, lo


def kernel(
    views, tiles, rf, rs, ra,
    est_hbm, img_ref, tf_hbm, ts_hbm, ta_hbm, out_ref,
    tf_ref, ts_ref, ta_ref, est, ext, planes, bplane, rplane, gplanes, left, left2, wconv, wcorr, pack, img, inverse, over, wide,
    img_send, img_recv, pk_send, pk_recv, local_sem, in_sem, h_send, h_recv, o_send, o_recv,
):
    nx, ny, nz = est_hbm.shape
    nf, ns, na = 2 * rf + 1, 2 * rs + 1, 2 * ra + 1
    frame = ny + 2 * PAD
    full = nx + 2 * rf
    v = lax.axis_index("view")
    t = lax.axis_index("tile")
    mid = pl.ds(PAD, ny)
    f32 = jnp.float32

    def inside(dt, dv):
        ok = None
        for d, at, count in ((dt, t, tiles), (dv, v, views)):
            if d:
                here = at + d < count if d > 0 else at + d >= 0
                ok = here if ok is None else jnp.logical_and(ok, here)
        return ok

    own = pltpu.make_async_copy(
        img_ref.at[0, :, pl.ds(pl.multiple_of(v * ny, 8), ny), :], img.at[v], local_sem
    )
    own.start()

    moves = [
        pltpu.make_async_copy(source, target, in_sem.at[n])
        for n, (source, target) in enumerate(
            ((tf_hbm, tf_ref), (ts_hbm, ts_ref), (ta_hbm, ta_ref))
        )
    ]
    for move in moves:
        move.start()
    est[0] = jnp.zeros(est.shape[1:], f32)

    barrier = pltpu.get_barrier_semaphore()
    for d in range(1, views):
        peer = lax.rem(v + d, views)
        pl.semaphore_signal(barrier, inc=1, device_id=(peer, t), device_id_type=MESH_ID)
    for dt, dv in DIRECTIONS:
        if dt:
            @pl.when(inside(dt, dv))
            def _(dt=dt, dv=dv):
                pl.semaphore_signal(
                    barrier, inc=1, device_id=(v + dv, t + dt), device_id_type=MESH_ID
                )

    start = pltpu.make_async_copy(est_hbm, est.at[0, pl.ds(rf, nx), mid, :], in_sem.at[3])
    start.start()
    pack[v] = jnp.zeros(pack.shape[1:], f32)
    rplane[...] = jnp.zeros(rplane.shape, f32)
    for move in moves:
        move.wait()
    for k in range(nf):
        pack[v, k : k + 1, :] = jnp.broadcast_to(tf_ref[0:1, k : k + 1], (1, nz))
    for k in range(ns):
        pack[v, nf + k : nf + k + 1, :] = jnp.broadcast_to(ts_ref[0:1, k : k + 1], (1, nz))
    pack[v, nf + ns : nf + ns + 1, 0:na] = ta_ref[...]
    start.wait()

    sides = jnp.where(t > 0, 1, 0) + jnp.where(t < tiles - 1, 1, 0)
    rows = 1 + jnp.where(v > 0, 1, 0) + jnp.where(v < views - 1, 1, 0)
    pl.semaphore_wait(barrier, views - 1 + sides * rows)

    def halo(n):
        dt, dv = DIRECTIONS[n]
        sp, dp, cp = {0: (rf, rf, nx), 1: (nx, 0, rf), -1: (rf, rf + nx, rf)}[dt]
        sr, dr, cr = {0: (PAD, PAD, ny), 1: (ny, 0, PAD), -1: (PAD, PAD + ny, PAD)}[dv]
        return pltpu.make_async_remote_copy(
            src_ref=est.at[0, pl.ds(sp, cp), pl.ds(sr, cr), :],
            dst_ref=est.at[0, pl.ds(dp, cp), pl.ds(dr, cr), :],
            send_sem=h_send.at[n], recv_sem=h_recv.at[n],
            device_id=(v + dv, t + dt), device_id_type=MESH_ID,
        )

    def region(it, n):
        dt, dv = DIRECTIONS[n]
        if it + 1 < ITERS:
            sp, dp, cp = {
                0: (0, 0, full), 1: (full - 2 * rf, 0, 2 * rf), -1: (0, full - 2 * rf, 2 * rf)
            }[dt]
            sr, dr, cr = {
                0: (0, 0, frame), 1: (ny, 0, 2 * PAD), -1: (0, ny, 2 * PAD)
            }[dv]
        else:
            sp, dp, cp = {0: (rf, rf, nx), 1: (rf + nx, rf, rf), -1: (0, nx, rf)}[dt]
            sr, dr, cr = {0: (PAD, PAD, ny), 1: (PAD + ny, PAD, PAD), -1: (0, ny, PAD)}[dv]
        return sp, dp, cp, sr, dr, cr

    def landing(it, n):
        return wide.at[it, n] if it + 1 < ITERS else over.at[n]

    def overhang(it, n):
        dt, dv = DIRECTIONS[n]
        sp, dp, cp, sr, dr, cr = region(it, n)
        return pltpu.make_async_remote_copy(
            src_ref=ext.at[it, pl.ds(sp, cp), pl.ds(sr, cr), :],
            dst_ref=landing(it, n).at[pl.ds(0, cp), pl.ds(0, cr), :],
            send_sem=o_send.at[it, n], recv_sem=o_recv.at[it, n],
            device_id=(v + dv, t + dt), device_id_type=MESH_ID,
        )

    def each(make, method, sending):
        for n, (dt, dv) in enumerate(DIRECTIONS):
            sign = 1 if sending else -1

            @pl.when(inside(sign * dt, sign * dv))
            def _(n=n):
                getattr(make(n), method)()

    def send_pack(d):
        peer = lax.rem(v + d, views)
        return pltpu.make_async_remote_copy(
            src_ref=pack.at[v], dst_ref=pack.at[v],
            send_sem=pk_send.at[d], recv_sem=pk_recv.at[views - d],
            device_id=(peer, t), device_id_type=MESH_ID,
        )

    def send_img(d):
        peer = lax.rem(v + d, views)
        return pltpu.make_async_remote_copy(
            src_ref=img_ref.at[0, :, pl.ds(pl.multiple_of(peer * ny, 8), ny), :],
            dst_ref=img.at[v],
            send_sem=img_send.at[d], recv_sem=img_recv.at[views - d],
            device_id=(peer, t), device_id_type=MESH_ID,
        )

    def arrived(buffer, sem, s, w):
        peer = lax.rem(v + s, views)
        pltpu.make_async_remote_copy(
            src_ref=buffer.at[w], dst_ref=buffer.at[w],
            send_sem=sem.at[s], recv_sem=sem.at[s],
            device_id=(peer, t), device_id_type=MESH_ID,
        ).wait_recv()

    for d in range(1, views):
        send_pack(d).start()
    each(halo, "start", True)
    for d in range(1, views):
        send_img(d).start()

    def prepare(s, w):
        @pl.when(s > 0)
        def _():
            arrived(pack, pk_recv, s, w)

        row = jnp.broadcast_to(pack[w, nf + ns : nf + ns + 1, :], (nz, nz))
        i = lax.broadcasted_iota(jnp.int32, (nz, nz), 0)
        j = lax.broadcasted_iota(jnp.int32, (nz, nz), 1)
        matrix = pltpu.roll(row, nz - ra, axis=1, stride=1, stride_axis=0)
        matrix = jnp.where(jnp.abs(i - j) <= ra, matrix, 0.0)
        for ref, m in ((wconv, matrix), (wcorr, matrix.T)):
            hi, lo = split(m)
            ref[w, 0:nz, :] = hi
            ref[w, nz : 2 * nz, :] = hi
            ref[w, 2 * nz : 3 * nz, :] = lo

    def taps(w):
        first = [pack[w, k : k + 1, :] for k in range(nf)]
        second = [pack[w, nf + k : nf + k + 1, :] for k in range(ns)]
        return first, second

    def spread(w):
        planes[...] = jnp.dot(left[...], wconv[w], preferred_element_type=f32).reshape(
            full, frame, nz
        )

    def blurred(x, first, second):
        bplane[x] = sum(first[k] * planes[x + nf - 1 - k] for k in range(nf))
        return sum(second[k] * bplane[x, pl.ds(PAD + rs - k, ny), :] for k in range(ns))

    def gather(x, ratio, second):
        rplane[x, pl.ds(2 * PAD, ny), :] = ratio
        gplanes[x] = sum(
            second[k] * rplane[x, pl.ds(PAD - rs + k, frame), :] for k in range(ns)
        )

    def finish(it, s, w, first):
        for x in range(full):
            total = sum(
                first[k] * gplanes[x + k - (nf - 1)]
                for k in range(nf)
                if 0 <= x + k - (nf - 1) < nx
            )
            hi, lo = split(total)
            rows = pl.ds(x * frame, frame)
            left2[rows, 0:nz] = hi
            left2[rows, nz : 2 * nz] = lo
            left2[rows, 2 * nz : 3 * nz] = hi
        part = jnp.dot(left2[...], wcorr[w], preferred_element_type=f32).reshape(
            full, frame, nz
        )

        @pl.when(s == 0)
        def _():
            ext[it] = part

        @pl.when(s > 0)
        def _():
            ext[it] = ext[it] + part

    def invert(s, carry):
        w = lax.rem(v + s, views)
        spread(w)
        first, second = taps(w)
        for x in range(nx):
            inverse[w, x] = 1.0 / blurred(x, first, second)
        return carry

    def correct(s, carry):
        w = lax.rem(v + s, views)

        @pl.when(s > 0)
        def _():
            arrived(img, img_recv, s, w)

        @pl.when(s == 0)
        def _():
            own.wait()

        first, second = taps(w)
        for x in range(nx):
            gather(x, img[w, x] * inverse[w, x], second)
        finish(0, s, w, first)
        return carry

    def both(it, s, carry):
        w = lax.rem(v + s, views)
        spread(w)
        first, second = taps(w)
        for x in range(nx):
            gather(x, img[w, x] / blurred(x, first, second), second)
        finish(it, s, w, first)
        return carry

    def weights(s, carry):
        prepare(s, lax.rem(v + s, views))
        return carry

    lax.fori_loop(0, views, weights, 0)
    each(halo, "wait_recv", False)
    for it in range(ITERS):
        hi, lo = split(est[it].reshape(full * frame, nz))
        left[:, 0:nz] = hi
        left[:, nz : 2 * nz] = lo
        left[:, 2 * nz : 3 * nz] = hi
        if it == 0:
            lax.fori_loop(0, views, invert, 0)
            lax.fori_loop(0, views, correct, 0)
        else:
            lax.fori_loop(0, views, functools.partial(both, it), 0)
        each(functools.partial(overhang, it), "start", True)
        last = it + 1 == ITERS
        if not last:
            est[it + 1] = ext[it]
        for n, (dt, dv) in enumerate(DIRECTIONS):
            @pl.when(inside(-dt, -dv))
            def _(n=n, it=it, last=last):
                overhang(it, n).wait_recv()
                _, dp, cp, _, dr, cr = region(it, n)
                to = ext.at[it] if last else est.at[it + 1]
                place = (pl.ds(dp, cp), pl.ds(dr, cr), slice(None))
                to[place] = to[place] + landing(it, n)[pl.ds(0, cp), pl.ds(0, cr), :]

        if last:
            for x in range(nx):
                out_ref[x] = est[it, rf + x, mid, :] * (ext[it, rf + x, mid, :] / views)
        else:
            est[it + 1] = est[it] * (est[it + 1] / views)

    each(halo, "wait_send", True)
    for it in range(ITERS):
        each(functools.partial(overhang, it), "wait_send", True)
    for d in range(1, views):
        send_pack(d).wait_send()
        send_img(d).wait_send()


def local(views, tiles, estimate, images, taps_first, taps_second, taps_axial):
    nx, ny, nz = estimate.shape
    rf, rs, ra = [(taps.shape[1] - 1) // 2 for taps in (taps_first, taps_second, taps_axial)]
    frame = ny + 2 * PAD
    full = nx + 2 * rf
    f32, bf16 = jnp.float32, jnp.bfloat16
    vmem = pl.BlockSpec(memory_space=pltpu.VMEM)
    dma = pltpu.SemaphoreType.DMA
    directions = len(DIRECTIONS)
    rows = -(-(2 * rf + 2 * rs + 3) // 8) * 8
    return pl.pallas_call(
        functools.partial(kernel, views, tiles, rf, rs, ra),
        out_shape=jax.ShapeDtypeStruct(estimate.shape, f32),
        in_specs=[pl.BlockSpec(memory_space=pltpu.HBM)] * 5,
        out_specs=vmem,
        scratch_shapes=[
            pltpu.VMEM(taps_first.shape, f32),
            pltpu.VMEM(taps_second.shape, f32),
            pltpu.VMEM(taps_axial.shape, f32),
            pltpu.VMEM((ITERS, full, frame, nz), f32),
            pltpu.VMEM((ITERS, full, frame, nz), f32),
            pltpu.VMEM((full, frame, nz), f32),
            pltpu.VMEM((nx, frame, nz), f32),
            pltpu.VMEM((nx, frame + 2 * PAD, nz), f32),
            pltpu.VMEM((nx, frame, nz), f32),
            pltpu.VMEM((full * frame, 3 * nz), bf16),
            pltpu.VMEM((full * frame, 3 * nz), bf16),
            pltpu.VMEM((views, 3 * nz, nz), bf16),
            pltpu.VMEM((views, 3 * nz, nz), bf16),
            pltpu.VMEM((views, rows, nz), f32),
            pltpu.VMEM((views, nx, ny, nz), f32),
            pltpu.VMEM((views, nx, ny, nz), f32),
            pltpu.VMEM((directions, nx, ny, nz), f32),
            pltpu.VMEM((ITERS - 1, directions, full, frame, nz), f32),
            dma((views,)), dma((views,)), dma((views,)), dma((views,)), dma, dma((4,)),
            dma((directions,)), dma((directions,)),
            dma((ITERS, directions)), dma((ITERS, directions)),
        ],
        compiler_params=pltpu.CompilerParams(
            collective_id=0, has_side_effects=True, vmem_limit_bytes=60 * 2**20
        ),
    )(estimate, images, taps_first, taps_second, taps_axial)


def solution(mesh):
    in_specs = (
        P("tile", "view", None),
        P("view", "tile", None, None),
        P("view", None),
        P("view", None),
        P("view", None),
    )
    out_specs = P("tile", "view", None)
    call = functools.partial(local, mesh.shape["view"], mesh.shape["tile"])
    return jax.shard_map(call, mesh=mesh, in_specs=in_specs, out_specs=out_specs, check_vma=False)
```

time: 46 us -> 41.7 us (0.907)
  local copies, waits for them, and re-layouts: 4.84 us -> 1.67 us
  Pallas kernels: 40.8 us -> 39.6 us
    unnamed x11 -> x1, local copies, waits for them, and re-layouts: 4.84 us -> 1.67 us
    pallas_call x1, Pallas kernels: 40.8 us -> 39.6 us  [local(): pl.pallas_call(functools.partial(kernel, views, tiles, rf, rs, ra), out_s...]
where the time goes in v2:
time: 41.7 us; the launch traced here: 41.3 us
  Pallas kernels  39.6 us (95%)
  local copies, waits for them, and re-layouts  1.67 us (4%)
    pallas_call x1, Pallas kernels, local(): pl.pallas_call(functools.partial(kernel, views, tiles, rf, rs, ra), out_s...  39.6 us
    unnamed x1, local copies, waits for them, and re-layouts  1.67 us

profile of v2, /device:TPU:1, one launch (start us, length us, event | category | flops | bytes accessed | tf_op | source)
XLA Modules:
  0.0 41.3 jit_solution(17246885426045083090)
XLA Ops:
  0.0 39.6 %shard_map.55 = f32[8,64,128]{2,1,0:T(8,128)} custom-call(f32[8,64,128]{2,1,0:T(8,128)} %est_hbm.1, f32[1,8,256,128]{3,2,1,0:T(8,128)} %img_ref.1, f32[1,5]{1,0:T(1,128)} %tf_hbm.1, f32[1,7]{1,0:T(1,128)} %ts_hbm.1, f32[1,33]{1,0:T(1,128)} %ta_hbm.1), custom_call_target="tpu_custom_call" | custom-call | tf_op jit(solution)/shard_map/pallas_call | solution.py:313
  39.7 1.7 %copy.7 = f32[8,64,128]{2,1,0:T(8,128)} copy(f32[8,64,128]{2,1,0:T(8,128)} %shard_map.55) | data formatting | bytes 524288

commit v3 on v2

--- a/solution.py
+++ b/solution.py
@@ -157,10 +157,10 @@
             device_id=(peer, t), device_id_type=MESH_ID,
         ).wait_recv()
 
-    for d in range(1, views):
+    for d in reversed(range(1, views)):
         send_pack(d).start()
     each(halo, "start", True)
-    for d in range(1, views):
+    for d in reversed(range(1, views)):
         send_img(d).start()
 
     def prepare(s, w):

time: 41.7 us -> 40.4 us (0.969)
  Pallas kernels: 39.6 us -> 38.5 us
    pallas_call x1, Pallas kernels: 39.6 us -> 38.5 us  [local(): pl.pallas_call(functools.partial(kernel, views, tiles, rf, rs, ra), out_s...]
where the time goes in v3:
time: 40.4 us; the launch traced here: 40.2 us
  Pallas kernels  38.5 us (95%)
  local copies, waits for them, and re-layouts  1.67 us (4%)
    pallas_call x1, Pallas kernels, local(): pl.pallas_call(functools.partial(kernel, views, tiles, rf, rs, ra), out_s...  38.5 us
    unnamed x1, local copies, waits for them, and re-layouts  1.67 us

profile of v3, /device:TPU:1, one launch (start us, length us, event | category | flops | bytes accessed | tf_op | source)
XLA Modules:
  0.0 40.2 jit_solution(12487125658784655159)
XLA Ops:
  0.0 38.5 %shard_map.55 = f32[8,64,128]{2,1,0:T(8,128)} custom-call(f32[8,64,128]{2,1,0:T(8,128)} %est_hbm.1, f32[1,8,256,128]{3,2,1,0:T(8,128)} %img_ref.1, f32[1,5]{1,0:T(1,128)} %tf_hbm.1, f32[1,7]{1,0:T(1,128)} %ts_hbm.1, f32[1,33]{1,0:T(1,128)} %ta_hbm.1), custom_call_target="tpu_custom_call" | custom-call | tf_op jit(solution)/shard_map/pallas_call | solution.py:313
  38.5 1.7 %copy.7 = f32[8,64,128]{2,1,0:T(8,128)} copy(f32[8,64,128]{2,1,0:T(8,128)} %shard_map.55) | data formatting | bytes 524288

commit v4 on v3

--- a/solution.py
+++ b/solution.py
@@ -82,6 +82,24 @@
     pack[v, nf + ns : nf + ns + 1, 0:na] = ta_ref[...]
     start.wait()
 
+    def prepare(s, w):
+        @pl.when(s > 0)
+        def _():
+            arrived(pack, pk_recv, s, w)
+
+        row = jnp.broadcast_to(pack[w, nf + ns : nf + ns + 1, :], (nz, nz))
+        i = lax.broadcasted_iota(jnp.int32, (nz, nz), 0)
+        j = lax.broadcasted_iota(jnp.int32, (nz, nz), 1)
+        matrix = pltpu.roll(row, nz - ra, axis=1, stride=1, stride_axis=0)
+        matrix = jnp.where(jnp.abs(i - j) <= ra, matrix, 0.0)
+        for ref, m in ((wconv, matrix), (wcorr, matrix.T)):
+            hi, lo = split(m)
+            ref[w, 0:nz, :] = hi
+            ref[w, nz : 2 * nz, :] = hi
+            ref[w, 2 * nz : 3 * nz, :] = lo
+
+    prepare(0, v)
+
     sides = jnp.where(t > 0, 1, 0) + jnp.where(t < tiles - 1, 1, 0)
     rows = 1 + jnp.where(v > 0, 1, 0) + jnp.where(v < views - 1, 1, 0)
     pl.semaphore_wait(barrier, views - 1 + sides * rows)
@@ -124,8 +142,9 @@
             device_id=(v + dv, t + dt), device_id_type=MESH_ID,
         )
 
-    def each(make, method, sending):
-        for n, (dt, dv) in enumerate(DIRECTIONS):
+    def each(make, method, sending, chosen=range(len(DIRECTIONS))):
+        for n in chosen:
+            dt, dv = DIRECTIONS[n]
             sign = 1 if sending else -1
 
             @pl.when(inside(sign * dt, sign * dv))
@@ -159,25 +178,10 @@
 
     for d in reversed(range(1, views)):
         send_pack(d).start()
-    each(halo, "start", True)
+    each(halo, "start", True, range(6))
     for d in reversed(range(1, views)):
         send_img(d).start()
-
-    def prepare(s, w):
-        @pl.when(s > 0)
-        def _():
-            arrived(pack, pk_recv, s, w)
-
-        row = jnp.broadcast_to(pack[w, nf + ns : nf + ns + 1, :], (nz, nz))
-        i = lax.broadcasted_iota(jnp.int32, (nz, nz), 0)
-        j = lax.broadcasted_iota(jnp.int32, (nz, nz), 1)
-        matrix = pltpu.roll(row, nz - ra, axis=1, stride=1, stride_axis=0)
-        matrix = jnp.where(jnp.abs(i - j) <= ra, matrix, 0.0)
-        for ref, m in ((wconv, matrix), (wcorr, matrix.T)):
-            hi, lo = split(m)
-            ref[w, 0:nz, :] = hi
-            ref[w, nz : 2 * nz, :] = hi
-            ref[w, 2 * nz : 3 * nz, :] = lo
+    each(halo, "start", True, range(6, 8))
 
     def taps(w):
         first = [pack[w, k : k + 1, :] for k in range(nf)]
@@ -261,7 +265,7 @@
         prepare(s, lax.rem(v + s, views))
         return carry
 
-    lax.fori_loop(0, views, weights, 0)
+    lax.fori_loop(1, views, weights, 0)
     each(halo, "wait_recv", False)
     for it in range(ITERS):
         hi, lo = split(est[it].reshape(full * frame, nz))

time: 40.4 us -> 40.3 us (level)
  no operation moved by 1% of the time
where the time goes in v4:
time: 40.3 us; the launch traced here: 40.2 us
  Pallas kernels  38.5 us (96%)
  local copies, waits for them, and re-layouts  1.67 us (4%)
    pallas_call x1, Pallas kernels, local(): pl.pallas_call(functools.partial(kernel, views, tiles, rf, rs, ra), out_s...  38.5 us
    unnamed x1, local copies, waits for them, and re-layouts  1.67 us

profile of v4, /device:TPU:1, one launch (start us, length us, event | category | flops | bytes accessed | tf_op | source)
XLA Modules:
  0.0 40.2 jit_solution(14486674562774842847)
XLA Ops:
  0.0 38.5 %shard_map.55 = f32[8,64,128]{2,1,0:T(8,128)} custom-call(f32[8,64,128]{2,1,0:T(8,128)} %est_hbm.1, f32[1,8,256,128]{3,2,1,0:T(8,128)} %img_ref.1, f32[1,5]{1,0:T(1,128)} %tf_hbm.1, f32[1,7]{1,0:T(1,128)} %ts_hbm.1, f32[1,33]{1,0:T(1,128)} %ta_hbm.1), custom_call_target="tpu_custom_call" | custom-call | tf_op jit(solution)/shard_map/pallas_call | solution.py:317
  38.5 1.7 %copy.7 = f32[8,64,128]{2,1,0:T(8,128)} copy(f32[8,64,128]{2,1,0:T(8,128)} %shard_map.55) | data formatting | bytes 524288
